TPU v7x, 512 devices: a whole 4x4x16 slice. The times are simulated.
512 devices in a mesh: tm: 32 (over z_lo, y, core), space: 16 (over x, z_hi).
Axes of the slice: x: 4, y: 4, z: 16 (z_hi: 4, z_lo: 4; z = z_hi * 4 + z_lo), core: 2. Of those that a mesh axis runs over, the one named last changes fastest.
Arguments:
- evecs: float32 [32, 2, 12288, 256], P('tm', None, 'space'), may hold values from -0.0546875 to 0.0546875
- solutions: float32 [32, 2, 12288, 512], P('tm', None, 'space'), may hold values from -6 to 6
- sink_time_weight: float32 [32, 32], P(None, 'tm'), may hold values from 0.1 to 1
- noise_source_vector: float32 [32, 2, 4, 256], P('tm'), may hold values from -6 to 6
- probe: float32 [32, 2, 4, 256], P('tm'), may hold values from -6 to 6
- dilution_spin_index: int32 [32, 4], P('tm'), may hold values from 0 to 3
- dilution_lace_index: int32 [32, 4], P('tm'), may hold values from 0 to 7
Outputs:
- smeared: float32 [32, 2, 16, 12288], P('tm', None, None, 'space')
All inputs are finite; a program needn't handle non-finite values.
Results may differ from a plain program's by a relative error of at most 0.000071.
Values sent between devices are 32-bit elements; how exact they have to be, the bound alone decides.
A program may use at most 64 MiB of HBM per device.

v0:
```python
import jax
import jax.numpy as jnp
from jax import lax
from jax.sharding import PartitionSpec as P

EIGEN_COUNT = 256
DILUTION_COUNT = 4
SPIN_COUNT = 4
LACE_CLASSES = 8


def in_blocks(value, dim, peers):
    shape = value.shape
    tiles = value.reshape(*shape[:dim], peers, shape[dim] // peers, *shape[dim + 1 :])
    return jnp.moveaxis(tiles, dim, 0)


def sent_and_summed(value, axis, dim):
    tiles = in_blocks(value, dim, lax.axis_size(axis))
    arrived = lax.all_to_all(tiles, axis, split_axis=0, concat_axis=0, tiled=True)
    return arrived.sum(axis=0)


def laid_out(tiles, dim):
    tiles = jnp.moveaxis(tiles, 0, dim)
    shape = tiles.shape
    return tiles.reshape(*shape[:dim], shape[dim] * shape[dim + 1], *shape[dim + 2 :])


def copy_for_each(value, axis):
    copies = jnp.broadcast_to(value, (lax.axis_size(axis), *value.shape))
    return lax.all_to_all(copies, axis, split_axis=0, concat_axis=0, tiled=True)


def gathered_copies(value, axis, dim):
    return laid_out(copy_for_each(value, axis), dim)


def row_dot(left, right):
    return lax.dot_general(
        left,
        right,
        (((0,), (0,)), ((), ())),
        precision=lax.Precision.HIGHEST,
        preferred_element_type=jnp.float32,
    )


def per_device(
    evecs,
    solutions,
    sink_time_weight,
    noise_source_vector,
    probe,
    dilution_spin_index,
    dilution_lace_index,
):
    hp = lax.Precision.HIGHEST
    vreal, vimag = (evecs[0, 0], evecs[0, 1])
    preal, pimag = (solutions[0, 0], solutions[0, 1])
    part_real = row_dot(vreal, preal) + row_dot(vimag, pimag)
    part_imag = row_dot(vreal, pimag) - row_dot(vimag, preal)
    partial_value = jnp.stack([part_real, part_imag])
    n_time = lax.axis_size("tm")
    sums = sent_and_summed(partial_value, "space", 1)
    eigen_modes = sums.shape[1]
    blocks = sums.reshape(2, eigen_modes, n_time, sums.shape[2] // n_time)
    received = lax.all_to_all(blocks, "tm", split_axis=2, concat_axis=2, tiled=True)
    weights = sink_time_weight[:, 0]
    summed_result = jnp.einsum("cntj,t->cnj", received, weights, precision=hp)
    summed_result = summed_result.reshape(2, eigen_modes, DILUTION_COUNT, SPIN_COUNT)
    vector_lanes = jnp.arange(EIGEN_COUNT, dtype=jnp.int32) % LACE_CLASSES
    lace_matches = (vector_lanes[None, :] == dilution_lace_index[0][:, None]).astype(jnp.float32)
    spin_matches = (
        jnp.arange(SPIN_COUNT, dtype=jnp.int32)[None, :] == dilution_spin_index[0][:, None]
    ).astype(jnp.float32)
    ereal, eimag = (noise_source_vector[0, 0], noise_source_vector[0, 1])
    qreal, qimag = (probe[0, 0], probe[0, 1])
    prod_real = ereal * qreal + eimag * qimag
    prod_imag = ereal * qimag - eimag * qreal
    w_real = jnp.einsum("km,sm->ks", lace_matches, prod_real, precision=hp) * spin_matches
    w_imag = jnp.einsum("km,sm->ks", lace_matches, prod_imag, precision=hp) * spin_matches
    y_real, y_imag = (summed_result[0], summed_result[1])
    z_real = jnp.einsum("nka,ks->nas", y_real, w_real, precision=hp) - jnp.einsum(
        "nka,ks->nas", y_imag, w_imag, precision=hp
    )
    z_imag = jnp.einsum("nka,ks->nas", y_real, w_imag, precision=hp) + jnp.einsum(
        "nka,ks->nas", y_imag, w_real, precision=hp
    )
    combined = jnp.stack(
        [
            z_real.reshape(eigen_modes, SPIN_COUNT * SPIN_COUNT),
            z_imag.reshape(eigen_modes, SPIN_COUNT * SPIN_COUNT),
        ]
    )
    combined = gathered_copies(combined, "space", 1)
    f_real = row_dot(combined[0], vreal.T) - row_dot(combined[1], vimag.T)
    f_imag = row_dot(combined[1], vreal.T) + row_dot(combined[0], vimag.T)
    return jnp.stack([f_real, f_imag])[None]


def solution(mesh):
    placed = (
        P("tm", None, "space", None),
        P("tm", None, "space", None),
        P(None, "tm"),
        P("tm", None, None, None),
        P("tm", None, None, None),
        P("tm", None),
        P("tm", None),
    )
    return jax.shard_map(
        per_device,
        mesh=mesh,
        in_specs=placed,
        out_specs=P("tm", None, None, "space"),
        check_vma=False,
    )
```

profile of v0, /device:TPU:1, one launch (start us, length us, event | category | flops | bytes accessed | tf_op | source)
XLA Modules:
  0.0 124.7 jit_solution(16228487466776213236)
XLA Ops:
  0.0 3.3 %fusion = f32[256,512]{1,0:T(8,128)S(1)} fusion(f32[1,2,768,512]{3,2,1,0:T(8,128)} %param.8, f32[1,2,768,256]{3,2,1,0:T(8,128)} %param.7), kind=kOutput, calls=%fused_computation | convolution fusion | flops 1207959552 | bytes 2883584 | tf_op jit(solution)/shard_map/dot_general | solution.py:40
  3.3 2.9 %fusion.2 = f32[256,512]{1,0:T(8,128)S(1)} fusion(f32[1,2,768,512]{3,2,1,0:T(8,128)} %param.8, f32[1,2,768,256]{3,2,1,0:T(8,128)S(1)} %copy-done), kind=kOutput, calls=%fused_computation.2 | convolution fusion | flops 1207959552 | bytes 2883584 | tf_op jit(solution)/shard_map/dot_general | solution.py:40
  6.2 1.5 %fusion.15 = f32[256,512]{1,0:T(8,128)S(1)} fusion(f32[256,512]{1,0:T(8,128)S(1)} %fusion, f32[1,2,768,512]{3,2,1,0:T(8,128)S(1)} %copy-done.1, f32[1,2,768,256]{3,2,1,0:T(8,128)S(1)} %copy-done), kind=kOutput, calls=%fused_computation.13 | convolution fusion | flops 1208090624 | bytes 3407872 | tf_op jit(solution)/shard_map/dot_general | solution.py:40
  7.7 1.5 %fusion.12 = f32[256,512]{1,0:T(8,128)S(1)} fusion(f32[256,512]{1,0:T(8,128)S(1)} %fusion.2, f32[1,2,768,512]{3,2,1,0:T(8,128)S(1)} %copy-done.1, f32[1,2,768,256]{3,2,1,0:T(8,128)S(1)} %copy-done), kind=kOutput, calls=%fused_computation.12 | convolution fusion | flops 1208090624 | bytes 3407872 | tf_op jit(solution)/shard_map/dot_general | solution.py:40
  9.2 0.1 maximum_bitcast_fusion
  9.3 68.0 %all_to_all.15 = f32[16,2,16,512]{3,2,1,0:T(8,128)S(1)} all-to-all(f32[16,2,16,512]{3,2,1,0:T(8,128)S(1)} %maximum_bitcast_fusion), channel_id=1, replica_groups=mesh['tm'=32,'space'=16] {'space'}, dimensions={0} | all-to-all | bytes 2097152 | tf_op jit(solution)/shard_map/all_to_all | solution.py:20
  77.4 0.1 reduce_sum.9
  77.5 0.2 reshape.35
  77.7 0.3 copy.59
  78.0 0.9 reshape.42
  78.9 13.7 %all-to-all-start.1 = ((f32[32,1,512]{2,1,0:T(1,128)}), f32[32,1,512]{2,1,0:T(1,128)S(1)}, u32[]{:S(2)}, u32[]{:S(2)}) async-start(f32[32,1,512]{2,1,0:T(1,128)} %reshape.42), calls=%async_computation.1 | async-start | bytes 131072 | tf_op jit(solution)/shard_map/all_to_all | solution.py:68
  92.6 0.2 fusion.20
  92.8 0.2 fusion.21
  92.9 7.3 %all-to-all-done.1 = f32[32,1,512]{2,1,0:T(1,128)S(1)} async-done(((f32[32,1,512]{2,1,0:T(1,128)}), f32[32,1,512]{2,1,0:T(1,128)S(1)}, u32[]{:S(2)}, u32[]{:S(2)}) %all-to-all-start.1) | async-done | bytes 65568 | tf_op jit(solution)/shard_map/all_to_all | solution.py:68
  100.3 0.5 broadcast.29
  100.8 0.8 reduce.2
  101.6 0.2 reshape.43
  101.8 0.1 multiply_reduce_fusion
  101.9 0.1 copy.48
  102.1 0.2 fusion.42
  102.3 0.2 fusion.44
  102.5 0.2 convolution_add_fusion.1
  102.7 0.2 convolution_subtract_fusion.1
  103.0 0.1 reshape.44
  103.2 16.8 %all_to_all.16 = f32[16,1,512]{2,1,0:T(1,128)S(1)} all-to-all(f32[16,1,512]{2,1,0:T(1,128)S(1)} %reshape.44), channel_id=1, replica_groups=mesh['tm'=32,'space'=16] {'space'}, dimensions={0} | all-to-all | bytes 65536 | tf_op jit(solution)/shard_map/all_to_all | solution.py:32
  120.0 0.7 reduce.3
  120.7 0.1 reshape.45
  120.9 0.8 fusion.26
  121.7 0.8 fusion.28
  122.4 0.8 fusion.18
  123.2 0.8 fusion.19
  124.0 0.7 maximum_bitcast_fusion.1
  (21 shorter events, 0.2 us)
Async XLA Ops:
  0.0 3.3 %copy-start = (f32[1,2,768,256]{3,2,1,0:T(8,128)S(1)}, f32[1,2,768,256]{3,2,1,0:T(8,128)}, u32[]{:S(2)}) copy-start(f32[1,2,768,256]{3,2,1,0:T(8,128)} %param.7) | copy-start | bytes 4718596
  0.0 6.2 %copy-start.1 = (f32[1,2,768,512]{3,2,1,0:T(8,128)S(1)}, f32[1,2,768,512]{3,2,1,0:T(8,128)}, u32[]{:S(2)}) copy-start(f32[1,2,768,512]{3,2,1,0:T(8,128)} %param.8) | copy-start | bytes 9437188
  77.4 15.2 %copy-start.3 = (f32[1,2,4,256]{3,2,1,0:T(4,128)S(1)}, f32[1,2,4,256]{3,2,1,0:T(4,128)}, u32[]{:S(2)}) copy-start(f32[1,2,4,256]{3,2,1,0:T(4,128)} %param.11) | copy-start | bytes 24580
  77.4 15.2 %copy-start.4 = (f32[1,2,4,256]{3,2,1,0:T(4,128)S(1)}, f32[1,2,4,256]{3,2,1,0:T(4,128)}, u32[]{:S(2)}) copy-start(f32[1,2,4,256]{3,2,1,0:T(4,128)} %param.10) | copy-start | bytes 24580
  77.4 15.2 %copy-start.5 = (s32[1,4]{1,0:T(1,128)S(1)}, s32[1,4]{1,0:T(1,128)}, u32[]{:S(2)}) copy-start(s32[1,4]{1,0:T(1,128)} %param.13) | copy-start | bytes 52
  77.4 15.2 %copy-start.6 = (s32[1,4]{1,0:T(1,128)S(1)}, s32[1,4]{1,0:T(1,128)}, u32[]{:S(2)}) copy-start(s32[1,4]{1,0:T(1,128)} %param.12) | copy-start | bytes 52
  77.5 24.3 %copy-start.2 = (f32[32,1]{0,1:T(1,128)S(1)}, f32[32,1]{0,1:T(1,128)}, u32[]{:S(2)}) copy-start(f32[32,1]{0,1:T(1,128)} %param.9) | copy-start | bytes 388
  78.9 21.4 %all-to-all-start.1 = ((f32[32,1,512]{2,1,0:T(1,128)}), f32[32,1,512]{2,1,0:T(1,128)S(1)}, u32[]{:S(2)}, u32[]{:S(2)}) async-start(f32[32,1,512]{2,1,0:T(1,128)} %reshape.42), calls=%async_computation.1 | async-start | bytes 131072 | tf_op jit(solution)/shard_map/all_to_all | solution.py:68
where the time goes:
time: 125 us
  blocking collectives  84.8 us (68%)
  starting transfers between devices  13.7 us (11%)
  matrix products  13.6 us (11%)
  waiting for transfers between devices  7.32 us (6%)
  local copies, waits for them, and re-layouts  2.64 us (2%)
  other arithmetic  2.46 us (2%)
    all_to_all x1, blocking collectives, sent_and_summed(): lax.all_to_all(tiles, axis, split_axis=0, concat_axis=0, tiled=True)  68 us
    all_to_all x1, blocking collectives, copy_for_each(): return lax.all_to_all(copies, axis, split_axis=0, concat_axis=0, tiled=True)  16.8 us
    all_to_all x1, starting transfers between devices, per_device(): lax.all_to_all(blocks, 'tm', split_axis=2, concat_axis=2, tiled=True)  13.7 us
    dot_general x8, matrix products, row_dot(): lax.dot_general(left, right, (((0,), (0,)), ((), ())), precision=lax.Prec...  12.4 us
    all_to_all x1, waiting for transfers between devices, per_device(): lax.all_to_all(blocks, 'tm', split_axis=2, concat_axis=2, tiled=True)  7.32 us
  transfers between devices with their start and end apart: 1, of which 1 were waited for; matrix products, arithmetic and copies ran while one was open for 0% of the time, Pallas kernels for 0%

commit v1 on v0

v1 whole, which is shorter than its diff:
```python
import jax
import jax.numpy as jnp
from jax import lax
from jax.experimental import pallas as pl
from jax.experimental.pallas import tpu as pltpu
from jax.sharding import PartitionSpec as P

F32 = jnp.float32
BF16 = jnp.bfloat16
MESH = pl.DeviceIdType.MESH

NX, NY, NC, NZH, NZL = 4, 4, 2, 4, 4
MODES = 256
HALF = 128
ROWS = 768
BLOCK = 16
LACE_CLASSES = 8
CHUNK_ZL = ((0, 3), (1, 2))


def ring(d, n):
    return min(d, n - d)


PLANE = sorted(
    [(dx, dy, dc) for dx in range(NX) for dy in range(NY) for dc in range(NC) if (dx, dy, dc) != (0, 0, 0)],
    key=lambda o: -(ring(o[0], NX) + ring(o[1], NY)),
)
N_PLANE = len(PLANE)
ZH_STEPS = (2, 1, 3, 0)


def two_halves(value):
    high = value.astype(BF16)
    return high, (value - high.astype(F32)).astype(BF16)


def dot(left, right):
    return lax.dot_general(left, right, (((1,), (0,)), ((), ())), preferred_element_type=F32)


def kernel(
    v_hbm, p_hbm, weight_hbm, noise_hbm, probe_hbm, spin_hbm, lace_hbm,
    out_ref,
    weight_ref, noise_ref, probe_ref, spin_ref, lace_ref,
    v_buf, p_buf, a_high, a_low, p_high, p_low, q_buf,
    s1, s1_sum, s2, y_all, w_rows, w_got,
    load_sem, small_sem, w_recv, s1_recv, s2_recv, y_recv, w_send, s1_send, s2_send, y_send,
):
    t = lax.axis_index("tm")
    s = lax.axis_index("space")
    core = lax.rem(t, NC)
    y = lax.rem(t // NC, NY)
    zl = t // (NC * NY)
    x = s // NZH
    zh = lax.rem(s, NZH)

    def device(x_, y_, zh_, zl_, c_):
        return ((zl_ * NY + y_) * NC + c_, x_ * NZH + zh_)

    small = []
    for n, (hbm, ref) in enumerate(
        (
            (weight_hbm, weight_ref),
            (noise_hbm.at[0], noise_ref),
            (probe_hbm.at[0], probe_ref),
            (spin_hbm, spin_ref),
            (lace_hbm, lace_ref),
        )
    ):
        small.append(pltpu.make_async_copy(hbm, ref, small_sem.at[n]))
    load_v = pltpu.make_async_copy(v_hbm.at[0], v_buf, load_sem.at[0])
    load_v.start()
    load_p = []
    for chunk in range(2):
        for i, zlp in enumerate(CHUNK_ZL[chunk]):
            load = pltpu.make_async_copy(
                p_hbm.at[0, :, :, pl.ds(zlp * HALF, HALF)],
                p_buf.at[:, :, pl.ds((chunk * 2 + i) * HALF, HALF)],
                load_sem.at[1 + chunk * 2 + i],
            )
            load.start()
            load_p.append(load)
    for load in small:
        load.start()

    barrier = pltpu.get_barrier_semaphore()
    for dx, dy, dc in PLANE:
        peer = device(lax.rem(x + dx, NX), lax.rem(y + dy, NY), zh, zl, lax.rem(core + dc, NC))
        pl.semaphore_signal(barrier, inc=1, device_id=peer, device_id_type=MESH)
    for dz in range(1, NZH * NZL):
        z_ = lax.rem(zh * NZL + zl + dz, NZH * NZL)
        peer = device(x, y, z_ // NZL, lax.rem(z_, NZL), core)
        pl.semaphore_signal(barrier, inc=1, device_id=peer, device_id_type=MESH)

    small[0].wait()
    n_t = NZL * NY * NC
    own = lax.broadcasted_iota(jnp.int32, (n_t, n_t), 0) == lax.broadcasted_iota(jnp.int32, (n_t, n_t), 1)
    column = jnp.sum(jnp.where(own, weight_ref[...], 0.0), axis=1, keepdims=True)
    w_rows[...] = jnp.broadcast_to(column, (n_t, HALF)).reshape(NZL, NY * NC, HALF)

    load_v.wait()
    rh, rl = two_halves(v_buf[0].T)
    ih, il = two_halves(v_buf[1].T)
    for ref, r_, i_ in ((a_high, rh, ih), (a_low, rl, il)):
        ref[:MODES, :ROWS] = r_
        ref[:MODES, ROWS:] = i_
        ref[MODES:, :ROWS] = -i_
        ref[MODES:, ROWS:] = r_

    def project(chunk):
        for i in range(2):
            load_p[chunk * 2 + i].wait()
        lanes = slice(chunk * MODES, (chunk + 1) * MODES)
        for c in range(2):
            high, low = two_halves(p_buf[c, :, lanes])
            p_high[c * ROWS : (c + 1) * ROWS, :] = high
            p_low[c * ROWS : (c + 1) * ROWS, :] = low
        ph = p_high[...]
        q = dot(a_high[...], ph) + dot(a_low[...], ph) + dot(a_high[...], p_low[...])
        for c in range(2):
            qt = q[c * MODES : (c + 1) * MODES, :].T
            for i in range(2):
                for y_ in range(NY):
                    for c_ in range(NC):
                        row = ((i * NY + y_) * NC + c_) * BLOCK
                        for h in range(2):
                            q_buf[chunk, c * 2 + h, y_, c_, i] = qt[row : row + BLOCK, h * HALF : (h + 1) * HALF]

    def scatter(chunk):
        for n, (dx, dy, dc) in enumerate(PLANE):
            x_, y_, c_ = lax.rem(x + dx, NX), lax.rem(y + dy, NY), lax.rem(core + dc, NC)
            pltpu.make_async_remote_copy(
                src_ref=q_buf.at[chunk, x_, y_, c_],
                dst_ref=s1.at[chunk, n],
                send_sem=s1_send,
                recv_sem=s1_recv.at[chunk],
                device_id=device(x_, y_, zh, zl, c_),
                device_id_type=MESH,
            ).start()

    project(0)
    pl.semaphore_wait(barrier, N_PLANE + NZH * NZL - 1)
    for n, dz in enumerate((1, NZH * NZL - 1, 2)):
        z_ = lax.rem(zh * NZL + zl + dz, NZH * NZL)
        zl_ = lax.rem(z_, NZL)
        pltpu.make_async_remote_copy(
            src_ref=w_rows.at[zl_],
            dst_ref=w_got.at[zl],
            send_sem=w_send,
            recv_sem=w_recv,
            device_id=device(x, y, z_ // NZL, zl_, core),
            device_id_type=MESH,
        ).start()
    scatter(0)
    project(1)
    scatter(1)

    w_got[zl] = w_rows[zl]

    for load in small[1:]:
        load.wait()
    er, ei = noise_ref[0], noise_ref[1]
    qr, qi = probe_ref[0], probe_ref[1]
    prod_real = er * qr + ei * qi
    prod_imag = er * qi - ei * qr
    lace_of = lax.rem(lax.broadcasted_iota(jnp.int32, (4, MODES), 1), LACE_CLASSES)
    spin_of = lax.broadcasted_iota(jnp.int32, (4, 1), 0)
    row = lax.broadcasted_iota(jnp.int32, (16, 16), 0)
    col = lax.broadcasted_iota(jnp.int32, (16, 16), 1)
    m_real = jnp.zeros((16, 16), F32)
    m_imag = jnp.zeros((16, 16), F32)
    for k in range(4):
        lace = (lace_of == lace_ref[0, k]).astype(F32)
        spin = (spin_of == spin_ref[0, k]).astype(F32)
        wr = jnp.sum(prod_real * lace, axis=1, keepdims=True) * spin
        wi = jnp.sum(prod_imag * lace, axis=1, keepdims=True) * spin
        here = (lax.div(col, 4) == k) & (lax.rem(col, 4) == lax.div(row, 4))
        m_real += jnp.where(here, jnp.concatenate([wr] * 4, axis=0), 0.0)
        m_imag += jnp.where(here, jnp.concatenate([wi] * 4, axis=0), 0.0)
    mix = jnp.concatenate(
        [jnp.concatenate([m_real, -m_imag], axis=1), jnp.concatenate([m_imag, m_real], axis=1)], axis=0
    )

    pltpu.make_async_copy(w_got.at[pl.ds(0, 3)], w_got.at[pl.ds(0, 3)], w_recv).wait()
    for chunk in range(2):
        pltpu.make_async_copy(s1.at[chunk], s1.at[chunk], s1_recv.at[chunk]).wait()
        for i, zlp in enumerate(CHUNK_ZL[chunk]):
            total = None
            for dy in range(NY):
                for dc in range(NC):
                    part = None
                    for dx in range(NX):
                        if (dx, dy, dc) == (0, 0, 0):
                            term = q_buf[chunk, x, y, core, i]
                        else:
                            term = s1[chunk, PLANE.index((dx, dy, dc)), i]
                        part = term if part is None else part + term
                    source = lax.rem(y + NY - dy, NY) * NC + lax.rem(core + dc, NC)
                    part = part * w_got[zlp, pl.ds(source, 1), :]
                    total = part if total is None else total + part
            s1_sum[chunk * 2 + i] = total
            for dzh in ZH_STEPS:
                zh_ = lax.rem(zh + dzh, NZH)

                def send(zh_=zh_, dzh=dzh, zlp=zlp, at=chunk * 2 + i):
                    pltpu.make_async_remote_copy(
                        src_ref=s1_sum.at[at],
                        dst_ref=s2.at[dzh * NZL + zl],
                        send_sem=s2_send,
                        recv_sem=s2_recv,
                        device_id=device(x, y, zh_, zlp, core),
                        device_id_type=MESH,
                    ).start()

                if dzh:
                    send()
                else:
                    pl.when(zl != zlp)(send)

                    @pl.when(zl == zlp)
                    def _(at=chunk * 2 + i):
                        s2[zl] = s1_sum[at]

    n_z = NZH * NZL - 1
    pltpu.make_async_copy(s2.at[pl.ds(0, n_z)], s2.at[pl.ds(0, n_z)], s2_recv).wait()
    total = s2[0]
    for n in range(1, n_z + 1):
        total = total + s2[n]
    y_all[x] = total
    for dx in (2, 1, 3):
        pltpu.make_async_remote_copy(
            src_ref=y_all.at[x],
            dst_ref=y_all.at[x],
            send_sem=y_send,
            recv_sem=y_recv,
            device_id=device(lax.rem(x + dx, NX), y, zh, zl, core),
            device_id_type=MESH,
        ).start()
    pltpu.make_async_copy(y_all.at[pl.ds(0, 3)], y_all.at[pl.ds(0, 3)], y_recv).wait()

    y_cat = jnp.concatenate(
        [
            jnp.concatenate([y_all[0], y_all[1]], axis=1),
            jnp.concatenate([y_all[2], y_all[3]], axis=1),
        ],
        axis=0,
    )
    z = lax.dot_general(
        mix, y_cat, (((1,), (0,)), ((), ())), precision=lax.Precision.HIGHEST, preferred_element_type=F32
    )
    z_high, z_low = two_halves(jnp.concatenate([z[:16], z[16:]], axis=1))
    both = dot(jnp.concatenate([z_high, z_low], axis=0), a_high[...])
    f = both[:16] + both[16:] + dot(z_high, a_low[...])
    out_ref[0, 0] = f[:, :ROWS]
    out_ref[0, 1] = f[:, ROWS:]

    pltpu.make_async_copy(w_got.at[pl.ds(0, 3)], w_got.at[pl.ds(0, 3)], w_send).wait()
    pltpu.make_async_copy(s1, s1, s1_send).wait()
    pltpu.make_async_copy(s2.at[pl.ds(0, n_z)], s2.at[pl.ds(0, n_z)], s2_send).wait()
    pltpu.make_async_copy(y_all.at[pl.ds(0, 3)], y_all.at[pl.ds(0, 3)], y_send).wait()


def per_device(evecs, solutions, weights, noise, probe, spin, lace):
    vmem = pl.BlockSpec(memory_space=pltpu.VMEM)
    hbm = pl.BlockSpec(memory_space=pltpu.HBM)
    dma = pltpu.SemaphoreType.DMA
    return pl.pallas_call(
        kernel,
        out_shape=jax.ShapeDtypeStruct((1, 2, BLOCK, ROWS), F32),
        in_specs=[hbm] * 7,
        out_specs=vmem,
        scratch_shapes=[
            pltpu.VMEM((1, NZL * NY * NC), F32),
            pltpu.VMEM((2, 4, MODES), F32),
            pltpu.VMEM((2, 4, MODES), F32),
            pltpu.SMEM((1, 4), jnp.int32),
            pltpu.SMEM((1, 4), jnp.int32),
            pltpu.VMEM((2, ROWS, MODES), F32),
            pltpu.VMEM((2, ROWS, 2 * MODES), F32),
            pltpu.VMEM((2 * MODES, 2 * ROWS), BF16),
            pltpu.VMEM((2 * MODES, 2 * ROWS), BF16),
            pltpu.VMEM((2 * ROWS, MODES), BF16),
            pltpu.VMEM((2 * ROWS, MODES), BF16),
            pltpu.VMEM((2, NX, NY, NC, 2, BLOCK, HALF), F32),
            pltpu.VMEM((2, N_PLANE, 2, BLOCK, HALF), F32),
            pltpu.VMEM((4, BLOCK, HALF), F32),
            pltpu.VMEM((NZH * NZL, BLOCK, HALF), F32),
            pltpu.VMEM((4, BLOCK, HALF), F32),
            pltpu.VMEM((NZL, NY * NC, HALF), F32),
            pltpu.VMEM((NZL, NY * NC, HALF), F32),
            dma((5,)), dma((5,)), dma, dma((2,)), dma, dma, dma, dma, dma, dma,
        ],
        compiler_params=pltpu.CompilerParams(
            collective_id=0, has_side_effects=True, vmem_limit_bytes=62 * 2**20
        ),
        cost_estimate=pl.CostEstimate(flops=2_500_000_000, bytes_accessed=4_900_000, transcendentals=0),
    )(evecs, solutions, weights.T, noise, probe, spin, lace)


def solution(mesh):
    placed = (
        P("tm", None, "space", None),
        P("tm", None, "space", None),
        P(None, "tm"),
        P("tm", None, None, None),
        P("tm", None, None, None),
        P("tm", None),
        P("tm", None),
    )
    return jax.shard_map(
        per_device,
        mesh=mesh,
        in_specs=placed,
        out_specs=P("tm", None, None, "space"),
        check_vma=False,
    )
```

time: 125 us -> 43.9 us (0.35)
  the two profiles are of different devices: /device:TPU:1 before, /device:TPU:32 now
where the time goes in v1:
time: 43.9 us; the launch traced here: 43.7 us
  Pallas kernels  42.2 us (96%)
  local copies, waits for them, and re-layouts  1.54 us (4%)
    pallas_call x1, Pallas kernels, per_device(): pl.pallas_call(kernel, out_shape=jax.ShapeDtypeStruct((1, 2, BLOCK, ROWS)...  42.2 us
    unnamed x1, local copies, waits for them, and re-layouts  1.54 us

profile of v1, /device:TPU:32, one launch (start us, length us, event | category | flops | bytes accessed | tf_op | source)
XLA Modules:
  0.0 43.7 jit_solution(282398971003446318)
XLA Ops:
  0.0 42.2 %shard_map.73 = f32[1,2,16,768]{3,2,1,0:T(8,128)} custom-call(f32[1,2,768,256]{3,2,1,0:T(8,128)} %v_hbm.1, f32[1,2,768,512]{3,2,1,0:T(8,128)} %p_hbm.1, f32[1,32]{1,0:T(1,128)} %bitcast.1, f32[1,2,4,256]{3,2,1,0:T(4,128)} %noise_hbm.1, f32[1,2,4,256]{3,2,1,0:T(4,128)} %probe_hbm.1, s32[1,4]{1,0:T(1,128)} %spin_hbm.1, s32[1,4]{1,0:T(1,128)} %lace_hbm.1), custom_call_target="tpu_custom_call" | custom-call | flops 2500000000 | bytes 4900000 | tf_op jit(solution)/shard_map/pallas_call | solution.py:268
  42.2 1.5 %copy.9 = f32[1,2,16,768]{3,2,1,0:T(8,128)} copy(f32[1,2,16,768]{3,2,1,0:T(8,128)} %shard_map.73) | data formatting | bytes 196608

commit v2 on v1

v2 whole, which is shorter than its diff:
```python
import jax
import jax.numpy as jnp
from jax import lax
from jax.experimental import pallas as pl
from jax.experimental.pallas import tpu as pltpu
from jax.sharding import PartitionSpec as P

F32 = jnp.float32
BF16 = jnp.bfloat16
MESH = pl.DeviceIdType.MESH

NX, NY, NC, NZH, NZL = 4, 4, 2, 4, 4
MODES = 256
HALF = 128
ROWS = 768
BLOCK = 16
LACE_CLASSES = 8


def ring(d, n):
    return min(d, n - d)


CHUNK_ZL = ((0, 1), (2, 3))
X_PEERS = sorted(range(1, NX), key=lambda d: -ring(d, NX))
YC_PEERS = sorted(
    [(dy, dc) for dy in range(NY) for dc in range(NC) if (dy, dc) != (0, 0)], key=lambda o: -ring(o[0], NY)
)
N_Z = NZH * NZL
FIRST_ZH, LAST_ZH = (0, 1), (2, 3)


def two_halves(value):
    high = value.astype(BF16)
    return high, (value - high.astype(F32)).astype(BF16)


def dot(left, right):
    return lax.dot_general(left, right, (((1,), (0,)), ((), ())), preferred_element_type=F32)


def kernel(
    v_hbm, p_hbm, weight_hbm, noise_hbm, probe_hbm, spin_hbm, lace_hbm,
    out_ref,
    weight_ref, noise_ref, probe_ref, spin_ref, lace_ref,
    v_buf, p_buf, v_t, p_high, p_low, qx_buf, qy_buf,
    x1, y1, x_sum, y_sum, y2, x2, s1_sum, s2, y_all, w_rows, w_got,
    load_sem, small_sem, w_recv, x1_recv, y1_recv, y2_recv, x2_recv, s2_recv, y_recv, send_sem, near_sem, far_sem,
):
    t = lax.axis_index("tm")
    s = lax.axis_index("space")
    core = lax.rem(t, NC)
    y = lax.rem(t // NC, NY)
    zl = t // (NC * NY)
    x = s // NZH
    zh = lax.rem(s, NZH)

    def device(x_, y_, zh_, zl_, c_):
        return ((zl_ * NY + y_) * NC + c_, x_ * NZH + zh_)

    z = zh * NZL + zl

    def z_peer(dz):
        z_ = z + dz
        return device(x, y, z_ // NZL, lax.rem(z_, NZL), core)

    def x_peer(dx):
        return device(lax.rem(x + dx, NX), y, zh, zl, core)

    def yc_peer(dy, dc):
        return device(x, lax.rem(y + dy, NY), zh, zl, lax.rem(core + dc, NC))

    small = []
    for n, (hbm, ref) in enumerate(
        (
            (weight_hbm, weight_ref),
            (noise_hbm.at[0], noise_ref),
            (probe_hbm.at[0], probe_ref),
            (spin_hbm, spin_ref),
            (lace_hbm, lace_ref),
        )
    ):
        small.append(pltpu.make_async_copy(hbm, ref, small_sem.at[n]))
    load_v = [pltpu.make_async_copy(v_hbm.at[0, c], v_buf.at[c], load_sem.at[c]) for c in range(2)]
    load_p = [
        pltpu.make_async_copy(
            p_hbm.at[0, :, :, pl.ds(chunk * MODES, MODES)],
            p_buf.at[:, :, pl.ds(chunk * MODES, MODES)],
            load_sem.at[2 + chunk],
        )
        for chunk in range(2)
    ]
    for load in load_v + load_p:
        load.start()
    for load in small:
        load.start()

    def keep_v(n, value):
        rows = slice(n * ROWS, (n + 1) * ROWS)
        v_t[:MODES, rows], v_t[MODES:, rows] = two_halves(value)

    barrier = pltpu.get_barrier_semaphore()
    for dx in X_PEERS:
        pl.semaphore_signal(barrier, inc=1, device_id=x_peer(dx), device_id_type=MESH)
    for dy, dc in YC_PEERS:
        pl.semaphore_signal(barrier, inc=1, device_id=yc_peer(dy, dc), device_id_type=MESH)
    for dz in range(1, N_Z):

        @pl.when(z + dz < N_Z)
        def _():
            pl.semaphore_signal(barrier, inc=1, device_id=z_peer(dz), device_id_type=MESH)

    small[0].wait()
    n_t = NZL * NY * NC
    own = lax.broadcasted_iota(jnp.int32, (n_t, n_t), 0) == lax.broadcasted_iota(jnp.int32, (n_t, n_t), 1)
    column = jnp.sum(jnp.where(own, weight_ref[...], 0.0), axis=1, keepdims=True)
    w_rows[...] = jnp.broadcast_to(column, (n_t, HALF)).reshape(NZL, NY * NC, HALF)

    load_v[0].wait()
    v_real = v_buf[0].T
    keep_v(0, v_real)
    load_v[1].wait()
    v_imag = v_buf[1].T
    keep_v(1, v_imag)
    keep_v(2, v_real - v_imag)

    def product(n, value):
        rows = slice(n * ROWS, (n + 1) * ROWS)
        p_high[rows, :], p_low[rows, :] = two_halves(value)
        both = dot(v_t[:, rows], p_high[rows, :])
        return both[:MODES] + both[MODES:] + dot(v_t[:MODES, rows], p_low[rows, :])

    def keep_q(chunk, c, q):
        qt = q.T
        for y_ in range(NY):
            for c_ in range(NC):
                for h in range(2):
                    lanes = slice(h * HALF, (h + 1) * HALF)
                    row = (y_ * NC + c_) * BLOCK
                    qx_buf[chunk, c * 2 + h, y_ * NC + c_] = qt[row : row + BLOCK, lanes]
                    row += HALF
                    qy_buf[chunk, y_ * NC + c_, c * 2 + h] = qt[row : row + BLOCK, lanes]

    def project(chunk):
        load_p[chunk].wait()
        lanes = slice(chunk * MODES, (chunk + 1) * MODES)
        p_real, p_imag = p_buf[0, :, lanes], p_buf[1, :, lanes]
        rr = product(0, p_real)
        ii = product(1, p_imag)
        keep_q(chunk, 0, rr + ii)
        keep_q(chunk, 1, product(2, p_real + p_imag) - rr + ii)

    def send(src, dst, send_sem, recv_sem, to):
        pltpu.make_async_remote_copy(
            src_ref=src, dst_ref=dst, send_sem=send_sem, recv_sem=recv_sem, device_id=to, device_id_type=MESH
        ).start()

    def yc_index(dy, dc):
        return lax.rem(y + dy, NY) * NC + lax.rem(core + dc, NC)

    def arrived(ref, sem):
        pltpu.make_async_copy(ref, ref, sem).wait()

    def scatter(chunk):
        for n in range(len(YC_PEERS)):
            dy, dc = YC_PEERS[n]
            send(qy_buf.at[chunk, yc_index(dy, dc)], y1.at[chunk, n], send_sem.at[1], y1_recv.at[chunk], yc_peer(dy, dc))
            if n < len(X_PEERS):
                dx = X_PEERS[n]
                send(qx_buf.at[chunk, lax.rem(x + dx, NX)], x1.at[chunk, n], send_sem.at[0], x1_recv.at[chunk], x_peer(dx))

    def weighted(zlp, own, others):
        total = own * w_got[zlp, pl.ds(y * NC + core, 1), :]
        for n, (dy, dc) in enumerate(YC_PEERS):
            source = lax.rem(y + NY - dy, NY) * NC + lax.rem(core + dc, NC)
            total = total + others[n] * w_got[zlp, pl.ds(source, 1), :]
        return total

    def across(chunk):
        arrived(x1.at[chunk], x1_recv.at[chunk])
        total = qx_buf[chunk, x]
        for n in range(len(X_PEERS)):
            total = total + x1[chunk, n]
        x_sum[chunk] = total
        for n, (dy, dc) in enumerate(YC_PEERS):
            send(x_sum.at[chunk, yc_index(dy, dc)], y2.at[chunk, n], send_sem.at[2], y2_recv.at[chunk], yc_peer(dy, dc))
        arrived(y1.at[chunk], y1_recv.at[chunk])
        zlp = CHUNK_ZL[chunk][1]
        for x_ in range(NX):
            y_sum[chunk, x_] = weighted(
                zlp, qy_buf[chunk, y * NC + core, x_], [y1[chunk, n, x_] for n in range(len(YC_PEERS))]
            )
        for n, dx in enumerate(X_PEERS):
            send(y_sum.at[chunk, lax.rem(x + dx, NX)], x2.at[chunk, n], send_sem.at[3], x2_recv.at[chunk], x_peer(dx))

    def along_z(chunk, i):
        zlp, at = CHUNK_ZL[chunk][i], chunk * 2 + i
        if i == 0:
            arrived(y2.at[chunk], y2_recv.at[chunk])
            total = weighted(zlp, x_sum[chunk, y * NC + core], [y2[chunk, n] for n in range(len(YC_PEERS))])
        else:
            arrived(x2.at[chunk], x2_recv.at[chunk])
            total = y_sum[chunk, x]
            for n in range(len(X_PEERS)):
                total = total + x2[chunk, n]
        s1_sum[at] = total

    def to_z(at, zh_):
        zlp = CHUNK_ZL[at // 2][at % 2]
        here = z == zh_ * NZL + zlp

        @pl.when(jnp.logical_not(here))
        def _():
            send(s1_sum.at[at], s2.at[z], send_sem.at[4], s2_recv, device(x, y, zh_, zlp, core))

        @pl.when(here)
        def _():
            s2[z] = s1_sum[at]

    project(0)
    pl.semaphore_wait(barrier, len(X_PEERS) + len(YC_PEERS) + z)
    for dz in range(1, NZL):

        @pl.when(dz <= zl)
        def _():
            pl.semaphore_signal(near_sem, inc=1, device_id=z_peer(-dz), device_id_type=MESH)
            send(w_rows.at[zl - dz], w_got.at[zl], send_sem.at[5], w_recv, z_peer(-dz))

    scatter(0)
    project(1)
    scatter(1)

    for dz in range(1, N_Z):

        @pl.when((dz > zl) & (dz <= z))
        def _():
            pl.semaphore_signal(far_sem, inc=1, device_id=z_peer(-dz), device_id_type=MESH)

    w_got[zl] = w_rows[zl]

    @pl.when(zl < NZL - 1)
    def _():
        pl.semaphore_wait(near_sem, NZL - 1 - zl)

    for dz in range(1, NZL):

        @pl.when(zl + dz < NZL)
        def _():
            send(w_rows.at[zl + dz], w_got.at[zl], send_sem.at[5], w_recv, z_peer(dz))


    for load in small[1:]:
        load.wait()
    er, ei = noise_ref[0], noise_ref[1]
    qr, qi = probe_ref[0], probe_ref[1]
    prod_real = er * qr + ei * qi
    prod_imag = er * qi - ei * qr
    lace_of = lax.rem(lax.broadcasted_iota(jnp.int32, (4, MODES), 1), LACE_CLASSES)
    spin_of = lax.broadcasted_iota(jnp.int32, (4, 1), 0)
    row = lax.broadcasted_iota(jnp.int32, (16, 16), 0)
    col = lax.broadcasted_iota(jnp.int32, (16, 16), 1)
    m_real = jnp.zeros((16, 16), F32)
    m_imag = jnp.zeros((16, 16), F32)
    for k in range(4):
        lace = (lace_of == lace_ref[0, k]).astype(F32)
        spin = (spin_of == spin_ref[0, k]).astype(F32)
        wr = jnp.sum(prod_real * lace, axis=1, keepdims=True) * spin
        wi = jnp.sum(prod_imag * lace, axis=1, keepdims=True) * spin
        here = (lax.div(col, 4) == k) & (lax.rem(col, 4) == lax.div(row, 4))
        m_real += jnp.where(here, jnp.concatenate([wr] * 4, axis=0), 0.0)
        m_imag += jnp.where(here, jnp.concatenate([wi] * 4, axis=0), 0.0)
    mix = jnp.concatenate(
        [jnp.concatenate([m_real, -m_imag], axis=1), jnp.concatenate([m_imag, m_real], axis=1)], axis=0
    )

    arrived(w_got.at[pl.ds(0, 3)], w_recv)
    across(0)
    across(1)

    @pl.when(zh < NZH - 1)
    def _():
        pl.semaphore_wait(far_sem, (NZH - 1 - zh) * NZL)

    for chunk in range(2):
        for i in range(2):
            along_z(chunk, i)
            for zh_ in FIRST_ZH:
                to_z(chunk * 2 + i, zh_)
    for at in range(4):
        for zh_ in LAST_ZH:
            to_z(at, zh_)

    n_z = NZH * NZL - 1
    arrived(s2.at[pl.ds(0, n_z)], s2_recv)
    total = s2[0]
    for n in range(1, n_z + 1):
        total = total + s2[n]
    y_all[x] = total
    for dx in X_PEERS:
        send(y_all.at[x], y_all.at[x], send_sem.at[6], y_recv, x_peer(dx))
    arrived(y_all.at[pl.ds(0, 3)], y_recv)

    y_cat = jnp.concatenate(
        [
            jnp.concatenate([y_all[0], y_all[1]], axis=1),
            jnp.concatenate([y_all[2], y_all[3]], axis=1),
        ],
        axis=0,
    )
    z_cat = lax.dot_general(
        mix, y_cat, (((1,), (0,)), ((), ())), precision=lax.Precision.HIGHEST, preferred_element_type=F32
    )
    z_high, z_low = two_halves(z_cat)
    z_both = jnp.concatenate([z_high, z_low], axis=0)
    f = []
    for n in range(2):
        rows = slice(n * ROWS, (n + 1) * ROWS)
        both = dot(z_both, v_t[:MODES, rows])
        f.append(both[:32] + both[32:] + dot(z_high, v_t[MODES:, rows]))
    out_ref[0, 0] = f[0][:16] - f[1][16:]
    out_ref[0, 1] = f[0][16:] + f[1][:16]

    for n, ref in enumerate(
        (x1, y1, y2, x2, s2.at[pl.ds(0, n_z)], w_got.at[pl.ds(0, 3)], y_all.at[pl.ds(0, 3)])
    ):
        arrived(ref, send_sem.at[n])


def per_device(evecs, solutions, weights, noise, probe, spin, lace):
    vmem = pl.BlockSpec(memory_space=pltpu.VMEM)
    hbm = pl.BlockSpec(memory_space=pltpu.HBM)
    dma = pltpu.SemaphoreType.DMA
    return pl.pallas_call(
        kernel,
        out_shape=jax.ShapeDtypeStruct((1, 2, BLOCK, ROWS), F32),
        in_specs=[hbm] * 7,
        out_specs=vmem,
        scratch_shapes=[
            pltpu.VMEM((1, NZL * NY * NC), F32),
            pltpu.VMEM((2, 4, MODES), F32),
            pltpu.VMEM((2, 4, MODES), F32),
            pltpu.SMEM((1, 4), jnp.int32),
            pltpu.SMEM((1, 4), jnp.int32),
            pltpu.VMEM((2, ROWS, MODES), F32),
            pltpu.VMEM((2, ROWS, 2 * MODES), F32),
            pltpu.VMEM((2 * MODES, 3 * ROWS), BF16),
            pltpu.VMEM((3 * ROWS, MODES), BF16),
            pltpu.VMEM((3 * ROWS, MODES), BF16),
            pltpu.VMEM((2, NX, NY * NC, BLOCK, HALF), F32),
            pltpu.VMEM((2, NY * NC, NX, BLOCK, HALF), F32),
            pltpu.VMEM((2, len(X_PEERS), NY * NC, BLOCK, HALF), F32),
            pltpu.VMEM((2, len(YC_PEERS), NX, BLOCK, HALF), F32),
            pltpu.VMEM((2, NY * NC, BLOCK, HALF), F32),
            pltpu.VMEM((2, NX, BLOCK, HALF), F32),
            pltpu.VMEM((2, len(YC_PEERS), BLOCK, HALF), F32),
            pltpu.VMEM((2, len(X_PEERS), BLOCK, HALF), F32),
            pltpu.VMEM((4, BLOCK, HALF), F32),
            pltpu.VMEM((NZH * NZL, BLOCK, HALF), F32),
            pltpu.VMEM((4, BLOCK, HALF), F32),
            pltpu.VMEM((NZL, NY * NC, HALF), F32),
            pltpu.VMEM((NZL, NY * NC, HALF), F32),
            dma((4,)), dma((5,)), dma, dma((2,)), dma((2,)), dma((2,)), dma((2,)), dma, dma, dma((7,)),
            pltpu.SemaphoreType.REGULAR, pltpu.SemaphoreType.REGULAR,
        ],
        compiler_params=pltpu.CompilerParams(
            collective_id=0, has_side_effects=True, vmem_limit_bytes=62 * 2**20
        ),
        cost_estimate=pl.CostEstimate(flops=2_500_000_000, bytes_accessed=4_900_000, transcendentals=0),
    )(evecs, solutions, weights.T, noise, probe, spin, lace)


def solution(mesh):
    placed = (
        P("tm", None, "space", None),
        P("tm", None, "space", None),
        P(None, "tm"),
        P("tm", None, None, None),
        P("tm", None, None, None),
        P("tm", None),
        P("tm", None),
    )
    return jax.shard_map(
        per_device,
        mesh=mesh,
        in_specs=placed,
        out_specs=P("tm", None, None, "space"),
        check_vma=False,
    )
```

time: 43.9 us -> 39.5 us (0.90)
  the two profiles are of different devices: /device:TPU:32 before, /device:TPU:96 now
where the time goes in v2:
time: 39.5 us; the launch traced here: 39.4 us
  Pallas kernels  37.9 us (96%)
  local copies, waits for them, and re-layouts  1.54 us (4%)
    pallas_call x1, Pallas kernels, per_device(): pl.pallas_call(kernel, out_shape=jax.ShapeDtypeStruct((1, 2, BLOCK, ROWS)...  37.9 us
    unnamed x1, local copies, waits for them, and re-layouts  1.54 us

profile of v2, /device:TPU:96, one launch (start us, length us, event | category | flops | bytes accessed | tf_op | source)
XLA Modules:
  0.0 39.4 jit_solution(3878958346381345309)
XLA Ops:
  0.0 37.9 %shard_map.73 = f32[1,2,16,768]{3,2,1,0:T(8,128)} custom-call(f32[1,2,768,256]{3,2,1,0:T(8,128)} %v_hbm.1, f32[1,2,768,512]{3,2,1,0:T(8,128)} %p_hbm.1, f32[1,32]{1,0:T(1,128)} %bitcast.1, f32[1,2,4,256]{3,2,1,0:T(4,128)} %noise_hbm.1, f32[1,2,4,256]{3,2,1,0:T(4,128)} %probe_hbm.1, s32[1,4]{1,0:T(1,128)} %spin_hbm.1, s32[1,4]{1,0:T(1,128)} %lace_hbm.1), custom_call_target="tpu_custom_call" | custom-call | flops 2500000000 | bytes 4900000 | tf_op jit(solution)/shard_map/pallas_call | solution.py:333
  37.9 1.5 %copy.9 = f32[1,2,16,768]{3,2,1,0:T(8,128)} copy(f32[1,2,16,768]{3,2,1,0:T(8,128)} %shard_map.73) | data formatting | bytes 196608

commit v3 on v2

--- a/solution.py
+++ b/solution.py
@@ -83,15 +83,21 @@
         small.append(pltpu.make_async_copy(hbm, ref, small_sem.at[n]))
     load_v = [pltpu.make_async_copy(v_hbm.at[0, c], v_buf.at[c], load_sem.at[c]) for c in range(2)]
     load_p = [
-        pltpu.make_async_copy(
-            p_hbm.at[0, :, :, pl.ds(chunk * MODES, MODES)],
-            p_buf.at[:, :, pl.ds(chunk * MODES, MODES)],
-            load_sem.at[2 + chunk],
-        )
+        [
+            pltpu.make_async_copy(
+                p_hbm.at[0, c, :, pl.ds(chunk * MODES, MODES)],
+                p_buf.at[c, :, pl.ds(chunk * MODES, MODES)],
+                load_sem.at[2 + chunk * 2 + c],
+            )
+            for c in range(2)
+        ]
         for chunk in range(2)
     ]
-    for load in load_v + load_p:
-        load.start()
+    for c in range(2):
+        load_v[c].start()
+        load_p[0][c].start()
+    for c in range(2):
+        load_p[1][c].start()
     for load in small:
         load.start()
 
@@ -115,14 +121,6 @@
     own = lax.broadcasted_iota(jnp.int32, (n_t, n_t), 0) == lax.broadcasted_iota(jnp.int32, (n_t, n_t), 1)
     column = jnp.sum(jnp.where(own, weight_ref[...], 0.0), axis=1, keepdims=True)
     w_rows[...] = jnp.broadcast_to(column, (n_t, HALF)).reshape(NZL, NY * NC, HALF)
-
-    load_v[0].wait()
-    v_real = v_buf[0].T
-    keep_v(0, v_real)
-    load_v[1].wait()
-    v_imag = v_buf[1].T
-    keep_v(1, v_imag)
-    keep_v(2, v_real - v_imag)
 
     def product(n, value):
         rows = slice(n * ROWS, (n + 1) * ROWS)
@@ -142,13 +140,22 @@
                     qy_buf[chunk, y_ * NC + c_, c * 2 + h] = qt[row : row + BLOCK, lanes]
 
     def project(chunk):
-        load_p[chunk].wait()
         lanes = slice(chunk * MODES, (chunk + 1) * MODES)
-        p_real, p_imag = p_buf[0, :, lanes], p_buf[1, :, lanes]
-        rr = product(0, p_real)
-        ii = product(1, p_imag)
+        if chunk == 0:
+            load_v[0].wait()
+            v_real = v_buf[0].T
+            keep_v(0, v_real)
+        load_p[chunk][0].wait()
+        rr = product(0, p_buf[0, :, lanes])
+        if chunk == 0:
+            load_v[1].wait()
+            v_imag = v_buf[1].T
+            keep_v(1, v_imag)
+            keep_v(2, v_real - v_imag)
+        load_p[chunk][1].wait()
+        ii = product(1, p_buf[1, :, lanes])
         keep_q(chunk, 0, rr + ii)
-        keep_q(chunk, 1, product(2, p_real + p_imag) - rr + ii)
+        keep_q(chunk, 1, product(2, p_buf[0, :, lanes] + p_buf[1, :, lanes]) - rr + ii)
 
     def send(src, dst, send_sem, recv_sem, to):
         pltpu.make_async_remote_copy(
@@ -284,10 +291,11 @@
     for chunk in range(2):
         for i in range(2):
             along_z(chunk, i)
-            for zh_ in FIRST_ZH:
-                to_z(chunk * 2 + i, zh_)
-    for at in range(4):
-        for zh_ in LAST_ZH:
+            to_z(chunk * 2 + i, 0)
+        for at in range(chunk * 2, chunk * 2 + 2):
+            to_z(at, 1)
+    for zh_ in range(2, NZH):
+        for at in range(4):
             to_z(at, zh_)
 
     n_z = NZH * NZL - 1
@@ -359,7 +367,7 @@
             pltpu.VMEM((4, BLOCK, HALF), F32),
             pltpu.VMEM((NZL, NY * NC, HALF), F32),
             pltpu.VMEM((NZL, NY * NC, HALF), F32),
-            dma((4,)), dma((5,)), dma, dma((2,)), dma((2,)), dma((2,)), dma((2,)), dma, dma, dma((7,)),
+            dma((6,)), dma((5,)), dma, dma((2,)), dma((2,)), dma((2,)), dma((2,)), dma, dma, dma((7,)),
             pltpu.SemaphoreType.REGULAR, pltpu.SemaphoreType.REGULAR,
         ],
         compiler_params=pltpu.CompilerParams(

time: 39.5 us -> 39.1 us (0.990)
  the two profiles are of different devices: /device:TPU:96 before, /device:TPU:64 now
where the time goes in v3:
time: 39.1 us; the launch traced here: 38.9 us
  Pallas kernels  37.4 us (96%)
  local copies, waits for them, and re-layouts  1.54 us (4%)
    pallas_call x1, Pallas kernels, per_device(): pl.pallas_call(kernel, out_shape=jax.ShapeDtypeStruct((1, 2, BLOCK, ROWS)...  37.4 us
    unnamed x1, local copies, waits for them, and re-layouts  1.54 us

profile of v3, /device:TPU:64, one launch (start us, length us, event | category | flops | bytes accessed | tf_op | source)
XLA Modules:
  0.0 38.9 jit_solution(13765238547321445995)
XLA Ops:
  0.0 37.4 %shard_map.73 = f32[1,2,16,768]{3,2,1,0:T(8,128)} custom-call(f32[1,2,768,256]{3,2,1,0:T(8,128)} %v_hbm.1, f32[1,2,768,512]{3,2,1,0:T(8,128)} %p_hbm.1, f32[1,32]{1,0:T(1,128)} %bitcast.1, f32[1,2,4,256]{3,2,1,0:T(4,128)} %noise_hbm.1, f32[1,2,4,256]{3,2,1,0:T(4,128)} %probe_hbm.1, s32[1,4]{1,0:T(1,128)} %spin_hbm.1, s32[1,4]{1,0:T(1,128)} %lace_hbm.1), custom_call_target="tpu_custom_call" | custom-call | flops 2500000000 | bytes 4900000 | tf_op jit(solution)/shard_map/pallas_call | solution.py:341
  37.4 1.5 %copy.9 = f32[1,2,16,768]{3,2,1,0:T(8,128)} copy(f32[1,2,16,768]{3,2,1,0:T(8,128)} %shard_map.73) | data formatting | bytes 196608

commit v4 on v3

--- a/solution.py
+++ b/solution.py
@@ -45,7 +45,7 @@
     weight_ref, noise_ref, probe_ref, spin_ref, lace_ref,
     v_buf, p_buf, v_t, p_high, p_low, qx_buf, qy_buf,
     x1, y1, x_sum, y_sum, y2, x2, s1_sum, s2, y_all, w_rows, w_got,
-    load_sem, small_sem, w_recv, x1_recv, y1_recv, y2_recv, x2_recv, s2_recv, y_recv, send_sem, near_sem, far_sem,
+    load_sem, small_sem, w_recv, x1_recv, y1_recv, y2_recv, x2_recv, s2_recv, y_recv, send_sem, near_sem, far_sem, out_buf, out_sem,
 ):
     t = lax.axis_index("tm")
     s = lax.axis_index("space")
@@ -96,20 +96,20 @@
     for c in range(2):
         load_v[c].start()
         load_p[0][c].start()
-    for c in range(2):
-        load_p[1][c].start()
-    for load in small:
-        load.start()
-
-    def keep_v(n, value):
-        rows = slice(n * ROWS, (n + 1) * ROWS)
-        v_t[:MODES, rows], v_t[MODES:, rows] = two_halves(value)
-
     barrier = pltpu.get_barrier_semaphore()
     for dx in X_PEERS:
         pl.semaphore_signal(barrier, inc=1, device_id=x_peer(dx), device_id_type=MESH)
     for dy, dc in YC_PEERS:
         pl.semaphore_signal(barrier, inc=1, device_id=yc_peer(dy, dc), device_id_type=MESH)
+    for c in range(2):
+        load_p[1][c].start()
+    for load in small:
+        load.start()
+
+    def keep_v(n, value):
+        rows = slice(n * ROWS, (n + 1) * ROWS)
+        v_t[:MODES, rows], v_t[MODES:, rows] = two_halves(value)
+
     for dz in range(1, N_Z):
 
         @pl.when(z + dz < N_Z)
@@ -320,29 +320,37 @@
     )
     z_high, z_low = two_halves(z_cat)
     z_both = jnp.concatenate([z_high, z_low], axis=0)
-    f = []
-    for n in range(2):
-        rows = slice(n * ROWS, (n + 1) * ROWS)
-        both = dot(z_both, v_t[:MODES, rows])
-        f.append(both[:32] + both[32:] + dot(z_high, v_t[MODES:, rows]))
-    out_ref[0, 0] = f[0][:16] - f[1][16:]
-    out_ref[0, 1] = f[0][16:] + f[1][:16]
+    leaving = []
+    for third in range(ROWS // MODES):
+        f = []
+        for n in range(2):
+            rows = slice(n * ROWS + third * MODES, n * ROWS + (third + 1) * MODES)
+            both = dot(z_both, v_t[:MODES, rows])
+            f.append(both[:32] + both[32:] + dot(z_high, v_t[MODES:, rows]))
+        out_buf[third, 0] = f[0][:16] - f[1][16:]
+        out_buf[third, 1] = f[0][16:] + f[1][:16]
+        copy = pltpu.make_async_copy(
+            out_buf.at[third], out_ref.at[0, :, :, pl.ds(third * MODES, MODES)], out_sem.at[third]
+        )
+        copy.start()
+        leaving.append(copy)
 
     for n, ref in enumerate(
         (x1, y1, y2, x2, s2.at[pl.ds(0, n_z)], w_got.at[pl.ds(0, 3)], y_all.at[pl.ds(0, 3)])
     ):
         arrived(ref, send_sem.at[n])
+    for copy in leaving:
+        copy.wait()
 
 
 def per_device(evecs, solutions, weights, noise, probe, spin, lace):
-    vmem = pl.BlockSpec(memory_space=pltpu.VMEM)
     hbm = pl.BlockSpec(memory_space=pltpu.HBM)
     dma = pltpu.SemaphoreType.DMA
     return pl.pallas_call(
         kernel,
         out_shape=jax.ShapeDtypeStruct((1, 2, BLOCK, ROWS), F32),
         in_specs=[hbm] * 7,
-        out_specs=vmem,
+        out_specs=hbm,
         scratch_shapes=[
             pltpu.VMEM((1, NZL * NY * NC), F32),
             pltpu.VMEM((2, 4, MODES), F32),
@@ -369,6 +377,7 @@
             pltpu.VMEM((NZL, NY * NC, HALF), F32),
             dma((6,)), dma((5,)), dma, dma((2,)), dma((2,)), dma((2,)), dma((2,)), dma, dma, dma((7,)),
             pltpu.SemaphoreType.REGULAR, pltpu.SemaphoreType.REGULAR,
+            pltpu.VMEM((ROWS // MODES, 2, BLOCK, MODES), F32), dma((ROWS // MODES,)),
         ],
         compiler_params=pltpu.CompilerParams(
             collective_id=0, has_side_effects=True, vmem_limit_bytes=62 * 2**20

time: 39.1 us -> 39.2 us (level)
  no operation moved by 1% of the time
where the time goes in v4:
time: 39.2 us; the launch traced here: 39.1 us
  Pallas kernels  37.5 us (96%)
  local copies, waits for them, and re-layouts  1.54 us (4%)
    pallas_call x1, Pallas kernels, per_device(): pl.pallas_call(kernel, out_shape=jax.ShapeDtypeStruct((1, 2, BLOCK, ROWS)...  37.5 us
    unnamed x1, local copies, waits for them, and re-layouts  1.54 us

profile of v4, /device:TPU:64, one launch (start us, length us, event | category | flops | bytes accessed | tf_op | source)
XLA Modules:
  0.0 39.1 jit_solution(8907549450370923131)
XLA Ops:
  0.0 37.5 %shard_map.73 = f32[1,2,16,768]{3,2,1,0:T(8,128)} custom-call(f32[1,2,768,256]{3,2,1,0:T(8,128)} %v_hbm.1, f32[1,2,768,512]{3,2,1,0:T(8,128)} %p_hbm.1, f32[1,32]{1,0:T(1,128)} %bitcast.1, f32[1,2,4,256]{3,2,1,0:T(4,128)} %noise_hbm.1, f32[1,2,4,256]{3,2,1,0:T(4,128)} %probe_hbm.1, s32[1,4]{1,0:T(1,128)} %spin_hbm.1, s32[1,4]{1,0:T(1,128)} %lace_hbm.1), custom_call_target="tpu_custom_call" | custom-call | flops 2500000000 | bytes 4900000 | tf_op jit(solution)/shard_map/pallas_call | solution.py:349
  37.6 1.5 %copy.9 = f32[1,2,16,768]{3,2,1,0:T(8,128)} copy(f32[1,2,16,768]{3,2,1,0:T(8,128)} %shard_map.73) | data formatting | bytes 196608

commit v5 on v3

--- a/solution.py
+++ b/solution.py
@@ -96,20 +96,20 @@
     for c in range(2):
         load_v[c].start()
         load_p[0][c].start()
-    for c in range(2):
-        load_p[1][c].start()
-    for load in small:
-        load.start()
-
-    def keep_v(n, value):
-        rows = slice(n * ROWS, (n + 1) * ROWS)
-        v_t[:MODES, rows], v_t[MODES:, rows] = two_halves(value)
-
     barrier = pltpu.get_barrier_semaphore()
     for dx in X_PEERS:
         pl.semaphore_signal(barrier, inc=1, device_id=x_peer(dx), device_id_type=MESH)
     for dy, dc in YC_PEERS:
         pl.semaphore_signal(barrier, inc=1, device_id=yc_peer(dy, dc), device_id_type=MESH)
+    for c in range(2):
+        load_p[1][c].start()
+    for load in small:
+        load.start()
+
+    def keep_v(n, value):
+        rows = slice(n * ROWS, (n + 1) * ROWS)
+        v_t[:MODES, rows], v_t[MODES:, rows] = two_halves(value)
+
     for dz in range(1, N_Z):
 
         @pl.when(z + dz < N_Z)

time: 39.1 us -> 39.1 us (level)
  no operation moved by 1% of the time
where the time goes in v5:
time: 39.1 us; the launch traced here: 38.9 us
  Pallas kernels  37.4 us (96%)
  local copies, waits for them, and re-layouts  1.54 us (4%)
    pallas_call x1, Pallas kernels, per_device(): pl.pallas_call(kernel, out_shape=jax.ShapeDtypeStruct((1, 2, BLOCK, ROWS)...  37.4 us
    unnamed x1, local copies, waits for them, and re-layouts  1.54 us

profile of v5, /device:TPU:64, one launch (start us, length us, event | category | flops | bytes accessed | tf_op | source)
XLA Modules:
  0.0 38.9 jit_solution(14552660698688580901)
XLA Ops:
  0.0 37.4 %shard_map.73 = f32[1,2,16,768]{3,2,1,0:T(8,128)} custom-call(f32[1,2,768,256]{3,2,1,0:T(8,128)} %v_hbm.1, f32[1,2,768,512]{3,2,1,0:T(8,128)} %p_hbm.1, f32[1,32]{1,0:T(1,128)} %bitcast.1, f32[1,2,4,256]{3,2,1,0:T(4,128)} %noise_hbm.1, f32[1,2,4,256]{3,2,1,0:T(4,128)} %probe_hbm.1, s32[1,4]{1,0:T(1,128)} %spin_hbm.1, s32[1,4]{1,0:T(1,128)} %lace_hbm.1), custom_call_target="tpu_custom_call" | custom-call | flops 2500000000 | bytes 4900000 | tf_op jit(solution)/shard_map/pallas_call | solution.py:341
  37.4 1.5 %copy.9 = f32[1,2,16,768]{3,2,1,0:T(8,128)} copy(f32[1,2,16,768]{3,2,1,0:T(8,128)} %shard_map.73) | data formatting | bytes 196608
